TPU v7x, 256 devices: a whole 4x4x8 slice. The times are simulated.
256 devices in a mesh: gx: 4 (over x), gy: 8 (over z), gz: 8 (over y, core).
Axes of the slice: x: 4, y: 4, z: 8, core: 2. Of those that a mesh axis runs over, the one named last changes fastest.
Arguments:
- solution: float32 [4, 8, 32, 64, 1024], P(None, None, 'gx', 'gy', 'gz'), may hold values from -6 to 6
- residual: float32 [4, 8, 32, 64, 1024], P(None, None, 'gx', 'gy', 'gz'), may hold values from -21 to 21
- permeability: float32 [4, 32, 64, 1024], P(None, 'gx', 'gy', 'gz'), may hold values from 0.1 to 1
- storage: float32 [4, 32, 64, 1024], P(None, 'gx', 'gy', 'gz'), may hold values from 0.5 to 2
- tissue_mask: int32 [32, 64, 1024], P('gx', 'gy', 'gz'), may hold values 0 or 1
- tissue_label: int32 [32, 64, 1024], P('gx', 'gy', 'gz'), may hold values from 0 to 2
- exchange_table: float32 [3, 6], replicated, may hold values from 0.2 to 1
Outputs:
- new_solution: float32 [4, 8, 32, 64, 1024], P(None, None, 'gx', 'gy', 'gz')
- new_residual: float32 [4, 8, 32, 64, 1024], P(None, None, 'gx', 'gy', 'gz')
- basis: float32 [4, 32, 32, 64, 1024], P(None, None, 'gx', 'gy', 'gz')
All inputs are finite; a program needn't handle non-finite values. No bound on the sum of `tissue_mask` on one device may be relied on, other than what follows from the above.
Results may differ from a plain program's by a relative error of at most 0.027.
Values sent between devices are 32-bit elements; how exact they have to be, the bound alone decides.
No kernel may reach another device: no remote copies, remote signals or barrier semaphores. Data moves between devices by JAX's collectives and lax.ppermute only.
A program may use at most 128 MiB of HBM per device.

v0:
```python
import jax
import jax.numpy as jnp
import numpy as np
from jax import lax
from jax.sharding import PartitionSpec as P

RHS = 8
S = 4
PAIRS = ((0, 1), (0, 2), (0, 3), (1, 2), (1, 3), (2, 3))
SHIFTS = (2.0, 14.0, 6.0, 10.0)
NEWTON_SCALE = 8.0
HIGHEST_PRECISION = lax.Precision.HIGHEST


def padded(cells, sides, width):
    for axis, dim in sides:
        count = lax.axis_size(axis)
        ends = count - 1
        head = lax.slice_in_dim(cells, 0, width, axis=dim)
        tail = lax.slice_in_dim(cells, cells.shape[dim] - width, cells.shape[dim], axis=dim)
        cells = jnp.concatenate(
            [
                lax.ppermute(tail, axis, [(i, (i + 1) % count) for i in range(ends)]),
                cells,
                lax.ppermute(head, axis, [((i + 1) % count, i) for i in range(ends)]),
            ],
            axis=dim,
        )
    return cells


def shifted(array, direction, offset):
    leading = array.ndim - 3
    index = [slice(None)] * leading
    for dimension in range(3):
        length = array.shape[leading + dimension]
        if dimension == direction:
            index.append(slice(offset, length - 2 + offset))
        else:
            index.append(slice(1, length - 1))
    return array[tuple(index)]


def interior(array):
    return shifted(array, 0, 1)


def stencil(field, perm_pad, mask_pad, store_pad, rate_pad):
    centre = interior(field)
    perm_mid = interior(perm_pad)
    mask_mid = interior(mask_pad)
    result = interior(store_pad)[:, None] * centre
    for direction in range(3):
        for offset in (0, 2):
            faces = (
                0.5
                * (perm_mid + shifted(perm_pad, direction, offset))
                * (mask_mid * shifted(mask_pad, direction, offset))
            )
            result = result + faces[:, None] * (centre - shifted(field, direction, offset))
    rate_mid = interior(rate_pad)
    pieces = [result[number] for number in range(4)]
    for number, pair in enumerate(PAIRS):
        flow = rate_mid[number] * (centre[pair[0]] - centre[pair[1]])
        pieces[pair[0]] = pieces[pair[0]] + flow
        pieces[pair[1]] = pieces[pair[1]] - flow
    return jnp.stack(pieces)


def apply_padded(field_pad, coeff_pad):
    return stencil(field_pad, coeff_pad[0:4], coeff_pad[14], coeff_pad[4:8], coeff_pad[8:14])


def build_coefficients(permeability, storage, tissue_mask, tissue_label, exchange_table):
    mask_float = tissue_mask.astype(jnp.float32)
    rates = jnp.zeros((6,) + tissue_mask.shape, jnp.float32)
    for level in range(3):
        weight = (tissue_label == level).astype(jnp.float32)
        rates = rates + exchange_table[level][:, None, None, None] * weight[None]
    rates = rates * mask_float[None]
    return jnp.concatenate([permeability, storage, rates, mask_float[None]], 0)


def newton_table(steps, rhs_count):
    table = np.zeros(((steps + 1) * rhs_count, steps * rhs_count), np.float32)
    for index in range(steps):
        table[
            index * rhs_count : (index + 1) * rhs_count, index * rhs_count : (index + 1) * rhs_count
        ] = SHIFTS[index] * np.eye(rhs_count)
        table[
            (index + 1) * rhs_count : (index + 2) * rhs_count,
            index * rhs_count : (index + 1) * rhs_count,
        ] = NEWTON_SCALE * np.eye(rhs_count)
    return jnp.asarray(table)


def local_gram(blocks):
    stacked = jnp.stack(blocks)
    flat = stacked.reshape(stacked.shape[0], stacked.shape[1], stacked.shape[2], -1)
    gram = jnp.einsum("kcjm,lcim->kjli", flat, flat, precision=HIGHEST_PRECISION)
    total = stacked.shape[0] * stacked.shape[2]
    return gram.reshape(total, total)


def lower_factor(matrix):
    extent = matrix.shape[0]
    positions = jnp.arange(extent)
    columns = []
    for col_index in range(extent):
        column = matrix[:, col_index]
        for inner in range(col_index):
            column = column - columns[inner] * columns[inner][col_index]
        pivot_value = jnp.sqrt(column[col_index])
        column = jnp.where(positions >= col_index, column / pivot_value, jnp.zeros_like(column))
        columns.append(column)
    return jnp.stack(columns, 1)


def lower_inverse(lower):
    extent = lower.shape[0]
    identity = jnp.eye(extent, dtype=lower.dtype)
    solved_rows = []
    for row_index in range(extent):
        current_row = identity[row_index]
        for inner in range(row_index):
            current_row = current_row - lower[row_index, inner] * solved_rows[inner]
        solved_rows.append(current_row / lower[row_index, row_index])
    return jnp.stack(solved_rows, 0)


def matmul(left, right):
    return jnp.dot(left, right, precision=HIGHEST_PRECISION)


def project(gram, steps, rhs_count):
    width = steps * rhs_count
    table = newton_table(steps, rhs_count)
    leading = gram[:width, :width]
    leading = 0.5 * (leading + leading.T)
    lower_inv = lower_inverse(lower_factor(leading))
    moment = matmul(gram[:width, :], table)
    moment = 0.5 * (moment + moment.T)
    projected = matmul(matmul(lower_inv, moment), lower_inv.T)
    projected = 0.5 * (projected + projected.T)
    right_part = matmul(lower_inv, gram[:width, :rhs_count])
    proj_inv = lower_inverse(lower_factor(projected))
    solved = matmul(proj_inv.T, matmul(proj_inv, right_part))
    inverse = lower_inv.T
    coeff = matmul(inverse, solved)
    extended = matmul(table, coeff)
    return (inverse, coeff, extended)


def finish(solution, residual, blocks, inverse, coeff, extended, steps, rhs_count):
    stacked = jnp.stack(blocks)
    flat = stacked.reshape(stacked.shape[0], stacked.shape[1], stacked.shape[2], -1)
    basis = jnp.einsum(
        "kcjm,kjq->cqm",
        flat[:steps],
        inverse.reshape(steps, rhs_count, -1),
        precision=HIGHEST_PRECISION,
    )
    basis = basis.reshape((stacked.shape[1], steps * rhs_count) + stacked.shape[3:])
    update = jnp.einsum(
        "kcjm,kji->cim",
        flat[:steps],
        coeff.reshape(steps, rhs_count, rhs_count),
        precision=HIGHEST_PRECISION,
    )
    image = jnp.einsum(
        "kcjm,kji->cim",
        flat,
        extended.reshape(steps + 1, rhs_count, rhs_count),
        precision=HIGHEST_PRECISION,
    )
    return (
        solution + update.reshape(solution.shape),
        residual - image.reshape(residual.shape),
        basis,
    )


def body(solution, residual, permeability, storage, tissue_mask, tissue_label, exchange_table):
    coefficients = build_coefficients(
        permeability, storage, tissue_mask, tissue_label, exchange_table
    )
    blocks = [residual]
    coeff_rim = padded(coefficients, (("gx", 1), ("gy", 2), ("gz", 3)), 1)
    current = residual
    for index in range(S):
        field_pad = padded(current, (("gx", 2), ("gy", 3), ("gz", 4)), 1)
        applied = apply_padded(field_pad, coeff_rim)
        current = (applied - SHIFTS[index] * current) / NEWTON_SCALE
        blocks.append(current)
    gram = lax.psum(local_gram(blocks), ("gx", "gy", "gz"))
    inverse, coeff, extended = project(gram, S, RHS)
    return finish(solution, residual, blocks, inverse, coeff, extended, S, RHS)


def solution(mesh):
    return jax.shard_map(
        body,
        mesh=mesh,
        in_specs=(
            P(None, None, "gx", "gy", "gz"),
            P(None, None, "gx", "gy", "gz"),
            P(None, "gx", "gy", "gz"),
            P(None, "gx", "gy", "gz"),
            P("gx", "gy", "gz"),
            P("gx", "gy", "gz"),
            P(),
        ),
        out_specs=(
            P(None, None, "gx", "gy", "gz"),
            P(None, None, "gx", "gy", "gz"),
            P(None, None, "gx", "gy", "gz"),
        ),
        check_vma=False,
    )
```

profile of v0, /device:TPU:1, one launch (start us, length us, event | category | flops | bytes accessed | tf_op | source)
XLA Modules:
  0.0 1804.4 jit_solution(12916086023873227692)
XLA Ops:
  157.0 5.2 collective-permute-start.20
  164.7 5.0 collective-permute-done.21
  182.9 6.5 collective-permute-start.22
  237.1 7.5 collective-permute-start.28
  262.7 8.3 fusion.4
  271.1 76.3 %psum.7 = f32[40,40]{1,0:T(8,128)S(1)} all-reduce(f32[40,40]{1,0:T(8,128)S(1)} %fusion.4), channel_id=1, replica_groups=mesh['gx'=4,'gy'=8,'gz'=8] {'gx','gy','gz'}, use_global_device_ids=true, to_apply=%region_0.0 | all-reduce | flops 1600 | bytes 12800 | tf_op jit(solution)/shard_map/psum | solution.py:195
  364.6 6.0 fusion.186
  404.2 5.7 multiply_subtract_fusion.51
  412.0 6.2 multiply_subtract_fusion.50
  420.2 6.8 multiply_subtract_fusion.49
  432.8 7.5 multiply_subtract_fusion.48
  442.4 6.1 fusion.177
  448.5 8.1 multiply_subtract_fusion.47
  458.7 8.7 multiply_subtract_fusion.46
  469.3 9.5 multiply_subtract_fusion.45
  480.9 9.6 multiply_subtract_fusion.44
  492.6 10.8 multiply_subtract_fusion.43
  505.4 10.9 multiply_subtract_fusion.42
  518.4 11.8 multiply_subtract_fusion.41
  532.2 12.5 multiply_subtract_fusion.40
  546.7 12.9 multiply_subtract_fusion.39
  561.5 6.0 fusion.168
  567.5 13.7 multiply_subtract_fusion.38
  583.1 14.4 multiply_subtract_fusion.37
  599.6 14.9 multiply_subtract_fusion.36
  616.4 15.8 multiply_subtract_fusion.35
  634.2 16.6 multiply_subtract_fusion.34
  652.9 16.6 multiply_subtract_fusion.33
  671.4 17.2 multiply_subtract_fusion.32
  690.8 18.4 %multiply_subtract_fusion.31 = f32[32]{0:T(128)S(1)} fusion(f32[32]{0:T(128)S(1)} %get-tuple-element.34, f32[]{:T(128)} %bitcast.543, f32[]{:T(128)} %bitcast.542, f32[]{:T(128)} %bitcast.541, f32[]{:T(128)} %bitcast.540, f32[]{:T(128)} %bitcast.539, f32[]{:T(128)} %bitcast.538, f32[]{:T(128)} %bitcast.537, f32[]{:T(128)} %bitcast.536, f32[]{:T(128)} %bitcast.535, ...), kind=kLoop, calls=%fused_computation.604 | loop fusion | flops 4608 | bytes 4196 | tf_op jit(solution)/shard_map/sub | solution.py:112
  711.1 19.0 %multiply_subtract_fusion.30 = f32[32]{0:T(128)S(1)} fusion(f32[32]{0:T(128)S(1)} %get-tuple-element.33, f32[]{:T(128)} %bitcast.576, f32[]{:T(128)} %bitcast.575, f32[]{:T(128)} %bitcast.574, f32[]{:T(128)} %bitcast.573, f32[]{:T(128)} %bitcast.572, f32[]{:T(128)} %bitcast.571, f32[]{:T(128)} %bitcast.570, f32[]{:T(128)} %bitcast.569, f32[]{:T(128)} %bitcast.568, ...), kind=kLoop, calls=%fused_computation.602 | loop fusion | flops 4768 | bytes 4332 | tf_op jit(solution)/shard_map/sub | solution.py:112
  731.9 65.1 %subtract_divide_fusion.49 = (f32[1,32]{1,0:T(1,128)S(1)}, f32[1,32]{1,0:T(1,128)S(1)}, f32[1,32]{1,0:T(1,128)S(1)}, f32[1,32]{1,0:T(1,128)S(1)}, f32[1,32]{1,0:...) fusion(f32[32,32]{1,0:T(8,128)S(1)} %fusion.206, ...), kind=kLoop, calls=%fused_computation.639 | loop fusion | flops 6272 | bytes 4004 | tf_op jit(solution)/shard_map/div | solution.py:127
  797.1 137.1 %subtract_divide_fusion.38 = (f32[1,32]{1,0:T(1,128)S(1)}, f32[1,32]{1,0:T(1,128)S(1)}, f32[1,32]{1,0:T(1,128)S(1)}, f32[1,32]{1,0:T(1,128)S(1)}, f32[1,32]{1,0:...) fusion(f32[1,32]{1,0:T(1,128)S(1)} %get-tuple-element.113, ...), kind=kLoop, calls=%fused_computation.617 | loop fusion | flops 13728 | bytes 5488 | tf_op jit(solution)/shard_map/div | solution.py:127
  934.2 127.1 %subtract_divide_fusion.31 = (f32[1,32]{1,0:T(1,128)S(1)}, f32[1,32]{1,0:T(1,128)S(1)}, f32[1,32]{1,0:T(1,128)S(1)}, f32[1,32]{1,0:T(1,128)S(1)}, f32[1,32]{1,0:...) fusion(f32[1,32]{1,0:T(1,128)S(1)} %get-tuple-element.102, f32[1,32]{1,0:T(1,128)S(1)} %get-tuple-element.103, ...), kind=kLoop, calls=%fused_computation.603 | loop fusion | flops 12768 | bytes 5804 | tf_op jit(solution)/shard_map/div | solution.py:127
  1079.1 6.2 fusion.154
  1118.9 5.7 multiply_subtract_fusion.21
  1126.6 6.2 multiply_subtract_fusion.20
  1134.9 6.8 multiply_subtract_fusion.19
  1147.2 7.4 multiply_subtract_fusion.18
  1156.8 6.1 fusion.145
  1162.9 8.1 multiply_subtract_fusion.17
  1173.1 8.7 multiply_subtract_fusion.16
  1183.7 9.5 multiply_subtract_fusion.15
  1195.3 9.6 multiply_subtract_fusion.14
  1207.0 10.8 multiply_subtract_fusion.13
  1219.8 10.9 multiply_subtract_fusion.12
  1232.8 11.8 multiply_subtract_fusion.11
  1246.6 12.5 multiply_subtract_fusion.10
  1261.1 12.9 multiply_subtract_fusion.9
  1275.9 6.0 fusion.136
  1281.9 13.7 multiply_subtract_fusion.8
  1297.5 14.4 multiply_subtract_fusion.7
  1314.0 14.9 multiply_subtract_fusion.6
  1330.8 15.8 multiply_subtract_fusion.5
  1348.7 16.6 multiply_subtract_fusion.4
  1367.3 16.6 multiply_subtract_fusion.3
  1385.8 17.2 multiply_subtract_fusion.2
  1405.2 18.4 %multiply_subtract_fusion.1 = f32[32]{0:T(128)S(1)} fusion(f32[32]{0:T(128)S(1)} %get-tuple-element.4, f32[]{:T(128)} %bitcast.1105, f32[]{:T(128)} %bitcast.1104, f32[]{:T(128)} %bitcast.1103, f32[]{:T(128)} %bitcast.1102, f32[]{:T(128)} %bitcast.1101, f32[]{:T(128)} %bitcast.1100, f32[]{:T(128)} %bitcast.1099, f32[]{:T(128)} %bitcast.1098, f32[]{:T(128)} %bitcast.1097, ...), kind=kLoop, calls=%fused_computation.543 | loop fusion | flops 4608 | bytes 4196 | tf_op jit(solution)/shard_map/sub | solution.py:112
  1425.5 19.0 %multiply_subtract_fusion = f32[32]{0:T(128)S(1)} fusion(f32[32]{0:T(128)S(1)} %get-tuple-element.3, f32[]{:T(128)} %bitcast.1138, f32[]{:T(128)} %bitcast.1137, f32[]{:T(128)} %bitcast.1136, f32[]{:T(128)} %bitcast.1135, f32[]{:T(128)} %bitcast.1134, f32[]{:T(128)} %bitcast.1133, f32[]{:T(128)} %bitcast.1132, f32[]{:T(128)} %bitcast.1131, f32[]{:T(128)} %bitcast.1130, ...), kind=kLoop, calls=%fused_computation.541 | loop fusion | flops 4768 | bytes 4332 | tf_op jit(solution)/shard_map/sub | solution.py:112
  1446.3 65.1 %subtract_divide_fusion.18 = (f32[1,32]{1,0:T(1,128)S(1)}, f32[1,32]{1,0:T(1,128)S(1)}, f32[1,32]{1,0:T(1,128)S(1)}, f32[1,32]{1,0:T(1,128)S(1)}, f32[1,32]{1,0:...) fusion(f32[32,32]{1,0:T(8,128)S(1)} %fusion.206, ...), kind=kLoop, calls=%fused_computation.578 | loop fusion | flops 6272 | bytes 4004 | tf_op jit(solution)/shard_map/div | solution.py:127
  1511.5 137.1 %subtract_divide_fusion.7 = (f32[1,32]{1,0:T(1,128)S(1)}, f32[1,32]{1,0:T(1,128)S(1)}, f32[1,32]{1,0:T(1,128)S(1)}, f32[1,32]{1,0:T(1,128)S(1)}, f32[1,32]{1,0:T...) fusion(f32[1,32]{1,0:T(1,128)S(1)} %get-tuple-element.81, ...), kind=kLoop, calls=%fused_computation.556 | loop fusion | flops 13728 | bytes 5488 | tf_op jit(solution)/shard_map/div | solution.py:127
  1648.6 127.1 %subtract_divide_fusion = (f32[1,32]{1,0:T(1,128)S(1)}, f32[1,32]{1,0:T(1,128)S(1)}, f32[1,32]{1,0:T(1,128)S(1)}, f32[1,32]{1,0:T(1,128)S(1)}, f32[1,32]{1,0:T(1...) fusion(f32[1,32]{1,0:T(1,128)S(1)} %get-tuple-element.70, f32[1,32]{1,0:T(1,128)S(1)} %get-tuple-element.71, ...), kind=kLoop, calls=%fused_computation.542 | loop fusion | flops 12768 | bytes 5804 | tf_op jit(solution)/shard_map/div | solution.py:127
  1776.6 11.7 fusion.131
  1788.3 7.5 fusion.3
  (555 shorter events, 399.2 us)
Async XLA Ops:
  0.6 8.7 copy-start
  2.2 55.6 %copy-start.49 = (f32[1,8,8,128]{3,2,1,0:T(8,128)}, f32[1,8,8,128]{3,2,1,0:T(8,128)S(1)}, u32[]{:S(2)}) copy-start(f32[1,8,8,128]{3,2,1,0:T(8,128)S(1)} %get-tuple-element.202) | copy-start | bytes 98308
  3.9 12.6 copy-start.9
  3.9 12.6 copy-start.10
  3.9 17.9 collective-permute-start
  8.0 13.8 collective-permute-start.1
  10.0 18.1 %collective-permute-start.7 = (f32[4,8,1,8,128]{4,1,3,2,0:T(8,128)S(1)}, f32[4,8,1,8,128]{4,1,3,2,0:T(8,128)S(1)}, u32[]{:S(2)}, u32[]{:S(2)}) collective-permute-start(f32[4,8,1,8,128]{4,1,3,2,0:T(8,128)S(1)} %get-tuple-element.169), channel_id=1, source_target_pairs={{64,0},{128,64},{192,128},{65,1},{129,65},{193,129},{66,2},{130,66... | collective-permute-start | bytes 393224 | tf_op jit(solution)/shard_map/ppermute | solution.py:25
  11.3 16.1 collective-permute-start.6
  16.6 74.7 %copy-start.32 = (f32[8,8,128]{2,1,0:T(8,128)}, f32[8,8,128]{2,1,0:T(8,128)S(1)}, u32[]{:S(2)}) copy-start(f32[8,8,128]{2,1,0:T(8,128)S(1)} %get-tuple-element.183) | copy-start | bytes 98308
  16.6 74.7 %copy-start.36 = (f32[8,8,128]{2,1,0:T(8,128)}, f32[8,8,128]{2,1,0:T(8,128)S(1)}, u32[]{:S(2)}) copy-start(f32[8,8,128]{2,1,0:T(8,128)S(1)} %get-tuple-element.184) | copy-start | bytes 98308
  16.6 74.7 %copy-start.40 = (f32[8,8,128]{2,1,0:T(8,128)}, f32[8,8,128]{2,1,0:T(8,128)S(1)}, u32[]{:S(2)}) copy-start(f32[8,8,128]{2,1,0:T(8,128)S(1)} %get-tuple-element.185) | copy-start | bytes 98308
  16.6 74.7 %copy-start.44 = (f32[8,8,128]{2,1,0:T(8,128)}, f32[8,8,128]{2,1,0:T(8,128)S(1)}, u32[]{:S(2)}) copy-start(f32[8,8,128]{2,1,0:T(8,128)S(1)} %get-tuple-element.188) | copy-start | bytes 98308
  21.8 36.0 %copy-start.48 = (f32[15,1,8,128]{3,2,1,0:T(8,128)}, f32[15,1,8,128]{3,2,1,0:T(8,128)S(1)}, u32[]{:S(2)}) copy-start(f32[15,1,8,128]{3,2,1,0:T(8,128)S(1)} %collective-permute-done.1) | copy-start | bytes 184324
  21.9 6.2 collective-permute-start.3
  23.2 5.6 collective-permute-start.2
  28.2 29.6 %copy-start.50 = (f32[15,10,1,128]{3,2,1,0:T(1,128)}, f32[15,10,1,128]{3,2,1,0:T(1,128)S(1)}, u32[]{:S(2)}) copy-start(f32[15,10,1,128]{3,2,1,0:T(1,128)S(1)} %copy.194) | copy-start | bytes 230404
  29.3 25.8 %copy-start.51 = (f32[15,10,1,128]{3,2,1,0:T(1,128)}, f32[15,10,1,128]{3,2,1,0:T(1,128)S(1)}, u32[]{:S(2)}) copy-start(f32[15,10,1,128]{3,2,1,0:T(1,128)S(1)} %copy.193) | copy-start | bytes 230404
  36.0 17.0 collective-permute-start.5
  40.1 10.8 collective-permute-start.4
  44.9 14.5 collective-permute-start.8
  49.6 9.8 collective-permute-start.9
  57.8 29.5 %copy-start.30 = (f32[4,8,8,128]{3,2,1,0:T(8,128)}, f32[4,8,8,128]{3,2,1,0:T(8,128)S(1)}, u32[]{:S(2)}) copy-start(f32[4,8,8,128]{3,2,1,0:T(8,128)S(1)} %get-tuple-element.175) | copy-start | bytes 393220
  57.8 29.5 %copy-start.31 = (f32[4,8,8,128]{3,2,1,0:T(8,128)}, f32[4,8,8,128]{3,2,1,0:T(8,128)S(1)}, u32[]{:S(2)}) copy-start(f32[4,8,8,128]{3,2,1,0:T(8,128)S(1)} %get-tuple-element.176) | copy-start | bytes 393220
  59.4 27.9 %copy-start.25 = (f32[4,8,8,128]{3,2,1,0:T(8,128)}, f32[4,8,8,128]{3,2,1,0:T(8,128)S(1)}, u32[]{:S(2)}) copy-start(f32[4,8,8,128]{3,2,1,0:T(8,128)S(1)} %get-tuple-element.182) | copy-start | bytes 393220
  71.0 12.2 collective-permute-start.11
  73.0 6.2 collective-permute-start.10
  78.0 9.3 copy-start.27
  78.0 9.3 copy-start.29
  78.0 9.3 copy-start.74
  78.0 9.3 copy-start.76
  92.8 5.8 collective-permute-start.12
  96.5 6.3 collective-permute-start.13
  98.7 16.6 copy-start.55
  102.8 12.5 copy-start.57
  102.8 7.7 collective-permute-start.14
  106.8 8.3 collective-permute-start.15
  110.5 4.7 copy-start.70
  121.4 9.9 collective-permute-start.16
  129.4 6.6 collective-permute-start.17
  139.2 4.3 copy-start.45
  139.2 4.3 copy-start.64
  147.9 5.8 collective-permute-start.18
  151.0 5.9 collective-permute-start.19
  153.6 9.9 copy-start.7
  153.6 16.1 copy-start.54
  156.9 12.8 copy-start.56
  157.0 7.8 collective-permute-start.20
  162.2 7.6 collective-permute-start.21
  164.7 5.0 copy-start.69
  180.9 15.0 collective-permute-start.23
  182.9 9.0 collective-permute-start.22
  189.4 10.7 copy-start.2
  189.4 10.7 copy-start.26
  189.4 10.7 copy-start.28
  205.7 3.9 collective-permute-start.24
  207.3 5.7 collective-permute-start.25
  209.6 14.3 copy-start.52
  213.0 11.0 copy-start.53
  213.0 7.2 collective-permute-start.26
  217.9 6.1 collective-permute-start.27
  235.1 15.8 collective-permute-start.29
  237.1 9.8 collective-permute-start.28
  262.7 169.8 %copy-start.77 = (f32[40,32]{1,0:T(8,128)S(1)}, f32[40,32]{1,0:T(8,128)}, u32[]{:S(2)}) copy-start(f32[40,32]{1,0:T(8,128)} %constant.92.clone) | copy-start | bytes 15364
  1776.6 11.7 copy-start.8
  (44 other events, 98.0 us)
where the time goes:
time: 1830 us; the launch traced here: 1800 us
  other arithmetic  1320 us (72%)
  local copies, waits for them, and re-layouts  207 us (11%)
  starting transfers between devices  90.5 us (5%)
  blocking collectives  76.3 us (4%)
  between operations  47.1 us (3%)
  waiting for transfers between devices  34.7 us (2%)
  matrix products  32.4 us (2%)
    div x6, other arithmetic, lower_inverse(): solved_rows.append(current_row / lower[row_index, row_index])  659 us
    sub x68, other arithmetic, lower_factor(): column = column - columns[inner] * columns[inner][col_index]  621 us
    psum x1, blocking collectives, body(): gram = lax.psum(local_gram(blocks), ('gx', 'gy', 'gz'))  76.3 us
    ppermute x15, starting transfers between devices, padded(): lax.ppermute(tail, axis, [(i, (i + 1) % count) for i in range(ends)])  65.7 us
    slice x64, local copies, waits for them, and re-layouts, lower_factor(): pivot_value = jnp.sqrt(column[col_index])  39.9 us
    slice x54, local copies, waits for them, and re-layouts, lower_inverse(): current_row = current_row - lower[row_index, inner] * solved_rows[inner]  38.3 us
  transfers between devices with their start and end apart: 30, of which 14 were waited for; matrix products, arithmetic and copies ran while one was open for 2% of the time, Pallas kernels for 0%

commit v1 on v0

--- a/solution.py
+++ b/solution.py
@@ -192,7 +192,7 @@
         applied = apply_padded(field_pad, coeff_rim)
         current = (applied - SHIFTS[index] * current) / NEWTON_SCALE
         blocks.append(current)
-    gram = lax.psum(local_gram(blocks), ("gx", "gy", "gz"))
+    gram = lax.psum(lax.psum(local_gram(blocks), "gx"), ("gy", "gz"))
     inverse, coeff, extended = project(gram, S, RHS)
     return finish(solution, residual, blocks, inverse, coeff, extended, S, RHS)
 

time: 1830 us -> 2010 us (1.098)
  blocking collectives: 76.3 us -> 253 us
    psum x1 -> x2, blocking collectives: 76.3 us -> 253 us  [body(): gram = lax.psum(lax.psum(local_gram(blocks), 'gx'), ('gy', 'gz'))]
where the time goes in v1:
time: 2010 us; the launch traced here: 1980 us
  other arithmetic  1320 us (66%)
  blocking collectives  253 us (13%)
  local copies, waits for them, and re-layouts  207 us (10%)
  starting transfers between devices  90.4 us (4%)
  between operations  47.2 us (2%)
  waiting for transfers between devices  34.7 us (2%)
  matrix products  32.4 us (2%)
    div x6, other arithmetic, lower_inverse(): solved_rows.append(current_row / lower[row_index, row_index])  659 us
    sub x68, other arithmetic, lower_factor(): column = column - columns[inner] * columns[inner][col_index]  621 us
    psum x2, blocking collectives, body(): gram = lax.psum(lax.psum(local_gram(blocks), 'gx'), ('gy', 'gz'))  253 us
    ppermute x15, starting transfers between devices, padded(): lax.ppermute(tail, axis, [(i, (i + 1) % count) for i in range(ends)])  65.7 us
  transfers between devices with their start and end apart: 30, of which 14 were waited for; matrix products, arithmetic and copies ran while one was open for 2% of the time, Pallas kernels for 0%

profile of v1, /device:TPU:1, one launch (start us, length us, event | category | flops | bytes accessed | tf_op | source)
XLA Modules:
  0.0 1980.9 jit_solution(4831626088186535690)
XLA Ops:
  156.9 5.2 collective-permute-start.20
  182.8 6.4 collective-permute-start.22
  237.1 7.5 collective-permute-start.28
  262.8 8.3 fusion.4
  271.1 11.2 psum.14
  282.3 241.7 %psum.15 = f32[40,40]{1,0:T(8,128)S(1)} all-reduce(f32[40,40]{1,0:T(8,128)S(1)} %psum.14), channel_id=1, replica_groups=mesh['gx'=4,'gy'=8,'gz'=8] {'gy','gz'}, use_global_device_ids=true, to_apply=%region_1.0 | all-reduce | flops 1600 | bytes 12800 | tf_op jit(solution)/shard_map/psum | solution.py:195
  541.1 5.8 fusion.186
  580.9 5.4 multiply_subtract_fusion.51
  588.4 6.3 multiply_subtract_fusion.50
  596.8 6.8 multiply_subtract_fusion.49
  609.2 7.6 multiply_subtract_fusion.48
  618.9 6.1 fusion.177
  624.9 7.8 multiply_subtract_fusion.47
  634.9 8.8 multiply_subtract_fusion.46
  645.8 9.0 multiply_subtract_fusion.45
  656.9 9.9 multiply_subtract_fusion.44
  668.9 10.7 multiply_subtract_fusion.43
  681.5 11.1 multiply_subtract_fusion.42
  694.6 11.8 multiply_subtract_fusion.41
  708.5 12.6 multiply_subtract_fusion.40
  723.2 13.1 multiply_subtract_fusion.39
  738.4 5.9 fusion.168
  744.4 13.8 multiply_subtract_fusion.38
  760.2 14.7 multiply_subtract_fusion.37
  776.8 14.8 multiply_subtract_fusion.36
  793.6 15.4 multiply_subtract_fusion.35
  810.9 16.5 multiply_subtract_fusion.34
  829.4 16.9 multiply_subtract_fusion.33
  848.2 17.4 multiply_subtract_fusion.32
  867.6 18.2 multiply_subtract_fusion.31
  887.8 18.9 multiply_subtract_fusion.30
  908.5 65.3 %subtract_divide_fusion.49 = (f32[1,32]{1,0:T(1,128)S(1)}, f32[1,32]{1,0:T(1,128)S(1)}, f32[1,32]{1,0:T(1,128)S(1)}, f32[1,32]{1,0:T(1,128)S(1)}, f32[1,32]{1,0:...) fusion(f32[32,32]{1,0:T(8,128)S(1)} %fusion.206, ...), kind=kLoop, calls=%fused_computation.639 | loop fusion | flops 6272 | bytes 4004 | tf_op jit(solution)/shard_map/div | solution.py:127
  973.9 137.1 %subtract_divide_fusion.38 = (f32[1,32]{1,0:T(1,128)S(1)}, f32[1,32]{1,0:T(1,128)S(1)}, f32[1,32]{1,0:T(1,128)S(1)}, f32[1,32]{1,0:T(1,128)S(1)}, f32[1,32]{1,0:...) fusion(f32[1,32]{1,0:T(1,128)S(1)} %get-tuple-element.113, ...), kind=kLoop, calls=%fused_computation.617 | loop fusion | flops 13728 | bytes 5488 | tf_op jit(solution)/shard_map/div | solution.py:127
  1111.0 126.8 %subtract_divide_fusion.31 = (f32[1,32]{1,0:T(1,128)S(1)}, f32[1,32]{1,0:T(1,128)S(1)}, f32[1,32]{1,0:T(1,128)S(1)}, f32[1,32]{1,0:T(1,128)S(1)}, f32[1,32]{1,0:...) fusion(f32[1,32]{1,0:T(1,128)S(1)} %get-tuple-element.102, f32[1,32]{1,0:T(1,128)S(1)} %get-tuple-element.103, ...), kind=kLoop, calls=%fused_computation.603 | loop fusion | flops 12768 | bytes 5804 | tf_op jit(solution)/shard_map/div | solution.py:127
  1255.5 6.0 fusion.154
  1295.5 5.4 multiply_subtract_fusion.21
  1303.0 6.3 multiply_subtract_fusion.20
  1311.3 6.8 multiply_subtract_fusion.19
  1323.5 7.6 multiply_subtract_fusion.18
  1333.2 6.1 fusion.145
  1339.2 7.8 multiply_subtract_fusion.17
  1349.2 8.8 multiply_subtract_fusion.16
  1360.1 9.0 multiply_subtract_fusion.15
  1371.2 9.9 multiply_subtract_fusion.14
  1383.2 10.7 multiply_subtract_fusion.13
  1395.8 11.1 multiply_subtract_fusion.12
  1408.9 11.8 multiply_subtract_fusion.11
  1422.8 12.6 multiply_subtract_fusion.10
  1437.5 13.1 multiply_subtract_fusion.9
  1452.7 5.9 fusion.136
  1458.7 13.8 multiply_subtract_fusion.8
  1474.5 14.7 multiply_subtract_fusion.7
  1491.1 14.8 multiply_subtract_fusion.6
  1507.9 15.4 multiply_subtract_fusion.5
  1525.2 16.5 multiply_subtract_fusion.4
  1543.7 16.9 multiply_subtract_fusion.3
  1562.5 17.4 multiply_subtract_fusion.2
  1581.8 18.2 multiply_subtract_fusion.1
  1602.1 18.9 multiply_subtract_fusion
  1622.8 65.3 %subtract_divide_fusion.18 = (f32[1,32]{1,0:T(1,128)S(1)}, f32[1,32]{1,0:T(1,128)S(1)}, f32[1,32]{1,0:T(1,128)S(1)}, f32[1,32]{1,0:T(1,128)S(1)}, f32[1,32]{1,0:...) fusion(f32[32,32]{1,0:T(8,128)S(1)} %fusion.206, ...), kind=kLoop, calls=%fused_computation.578 | loop fusion | flops 6272 | bytes 4004 | tf_op jit(solution)/shard_map/div | solution.py:127
  1688.2 137.1 %subtract_divide_fusion.7 = (f32[1,32]{1,0:T(1,128)S(1)}, f32[1,32]{1,0:T(1,128)S(1)}, f32[1,32]{1,0:T(1,128)S(1)}, f32[1,32]{1,0:T(1,128)S(1)}, f32[1,32]{1,0:T...) fusion(f32[1,32]{1,0:T(1,128)S(1)} %get-tuple-element.81, ...), kind=kLoop, calls=%fused_computation.556 | loop fusion | flops 13728 | bytes 5488 | tf_op jit(solution)/shard_map/div | solution.py:127
  1825.3 126.8 %subtract_divide_fusion = (f32[1,32]{1,0:T(1,128)S(1)}, f32[1,32]{1,0:T(1,128)S(1)}, f32[1,32]{1,0:T(1,128)S(1)}, f32[1,32]{1,0:T(1,128)S(1)}, f32[1,32]{1,0:T(1...) fusion(f32[1,32]{1,0:T(1,128)S(1)} %get-tuple-element.70, f32[1,32]{1,0:T(1,128)S(1)} %get-tuple-element.71, ...), kind=kLoop, calls=%fused_computation.542 | loop fusion | flops 12768 | bytes 5804 | tf_op jit(solution)/shard_map/div | solution.py:127
  1953.0 11.7 fusion.131
  1964.7 7.5 fusion.3
  (556 shorter events, 404.5 us)
Async XLA Ops:
  0.6 8.7 copy-start
  2.2 55.6 %copy-start.49 = (f32[1,8,8,128]{3,2,1,0:T(8,128)}, f32[1,8,8,128]{3,2,1,0:T(8,128)S(1)}, u32[]{:S(2)}) copy-start(f32[1,8,8,128]{3,2,1,0:T(8,128)S(1)} %get-tuple-element.202) | copy-start | bytes 98308
  3.9 12.6 copy-start.9
  3.9 12.6 copy-start.10
  3.9 17.9 collective-permute-start
  8.0 13.8 collective-permute-start.1
  10.0 18.1 collective-permute-start.7
  11.3 16.1 collective-permute-start.6
  16.6 74.7 %copy-start.32 = (f32[8,8,128]{2,1,0:T(8,128)}, f32[8,8,128]{2,1,0:T(8,128)S(1)}, u32[]{:S(2)}) copy-start(f32[8,8,128]{2,1,0:T(8,128)S(1)} %get-tuple-element.183) | copy-start | bytes 98308
  16.6 74.7 %copy-start.36 = (f32[8,8,128]{2,1,0:T(8,128)}, f32[8,8,128]{2,1,0:T(8,128)S(1)}, u32[]{:S(2)}) copy-start(f32[8,8,128]{2,1,0:T(8,128)S(1)} %get-tuple-element.184) | copy-start | bytes 98308
  16.6 74.7 %copy-start.40 = (f32[8,8,128]{2,1,0:T(8,128)}, f32[8,8,128]{2,1,0:T(8,128)S(1)}, u32[]{:S(2)}) copy-start(f32[8,8,128]{2,1,0:T(8,128)S(1)} %get-tuple-element.185) | copy-start | bytes 98308
  16.6 74.7 %copy-start.44 = (f32[8,8,128]{2,1,0:T(8,128)}, f32[8,8,128]{2,1,0:T(8,128)S(1)}, u32[]{:S(2)}) copy-start(f32[8,8,128]{2,1,0:T(8,128)S(1)} %get-tuple-element.188) | copy-start | bytes 98308
  21.8 36.0 %copy-start.48 = (f32[15,1,8,128]{3,2,1,0:T(8,128)}, f32[15,1,8,128]{3,2,1,0:T(8,128)S(1)}, u32[]{:S(2)}) copy-start(f32[15,1,8,128]{3,2,1,0:T(8,128)S(1)} %collective-permute-done.1) | copy-start | bytes 184324
  21.9 6.2 collective-permute-start.3
  23.2 5.6 collective-permute-start.2
  28.2 29.6 %copy-start.50 = (f32[15,10,1,128]{3,2,1,0:T(1,128)}, f32[15,10,1,128]{3,2,1,0:T(1,128)S(1)}, u32[]{:S(2)}) copy-start(f32[15,10,1,128]{3,2,1,0:T(1,128)S(1)} %copy.194) | copy-start | bytes 230404
  29.3 25.8 %copy-start.51 = (f32[15,10,1,128]{3,2,1,0:T(1,128)}, f32[15,10,1,128]{3,2,1,0:T(1,128)S(1)}, u32[]{:S(2)}) copy-start(f32[15,10,1,128]{3,2,1,0:T(1,128)S(1)} %copy.193) | copy-start | bytes 230404
  36.0 16.9 collective-permute-start.5
  40.1 10.8 collective-permute-start.4
  44.9 14.4 collective-permute-start.8
  49.6 9.8 collective-permute-start.9
  57.8 29.4 %copy-start.30 = (f32[4,8,8,128]{3,2,1,0:T(8,128)}, f32[4,8,8,128]{3,2,1,0:T(8,128)S(1)}, u32[]{:S(2)}) copy-start(f32[4,8,8,128]{3,2,1,0:T(8,128)S(1)} %get-tuple-element.175) | copy-start | bytes 393220
  57.8 29.4 %copy-start.31 = (f32[4,8,8,128]{3,2,1,0:T(8,128)}, f32[4,8,8,128]{3,2,1,0:T(8,128)S(1)}, u32[]{:S(2)}) copy-start(f32[4,8,8,128]{3,2,1,0:T(8,128)S(1)} %get-tuple-element.176) | copy-start | bytes 393220
  59.4 27.9 %copy-start.25 = (f32[4,8,8,128]{3,2,1,0:T(8,128)}, f32[4,8,8,128]{3,2,1,0:T(8,128)S(1)}, u32[]{:S(2)}) copy-start(f32[4,8,8,128]{3,2,1,0:T(8,128)S(1)} %get-tuple-element.182) | copy-start | bytes 393220
  71.0 12.2 collective-permute-start.11
  72.9 6.2 collective-permute-start.10
  77.9 9.3 copy-start.27
  78.0 9.3 copy-start.29
  78.0 9.3 copy-start.74
  78.0 9.3 copy-start.76
  92.8 5.8 collective-permute-start.12
  96.4 6.3 collective-permute-start.13
  98.6 16.6 copy-start.55
  102.7 12.5 copy-start.57
  102.8 7.7 collective-permute-start.14
  106.8 8.3 collective-permute-start.15
  110.5 4.7 copy-start.70
  121.4 9.9 collective-permute-start.16
  129.4 6.6 collective-permute-start.17
  139.2 4.3 copy-start.45
  139.2 4.3 copy-start.64
  147.9 5.8 collective-permute-start.18
  151.0 5.9 collective-permute-start.19
  153.6 9.9 copy-start.7
  153.6 16.1 copy-start.54
  156.9 12.8 copy-start.56
  156.9 7.8 collective-permute-start.20
  162.2 7.6 collective-permute-start.21
  164.7 5.0 copy-start.69
  180.9 15.0 collective-permute-start.23
  182.8 9.0 collective-permute-start.22
  189.3 10.7 copy-start.2
  189.3 10.7 copy-start.26
  189.3 10.7 copy-start.28
  205.7 4.0 collective-permute-start.24
  207.3 5.7 collective-permute-start.25
  209.6 14.3 copy-start.52
  213.0 11.0 copy-start.53
  213.0 7.2 collective-permute-start.26
  217.9 6.1 collective-permute-start.27
  235.2 15.8 collective-permute-start.29
  237.1 9.8 collective-permute-start.28
  262.8 346.2 %copy-start.77 = (f32[40,32]{1,0:T(8,128)S(1)}, f32[40,32]{1,0:T(8,128)}, u32[]{:S(2)}) copy-start(f32[40,32]{1,0:T(8,128)} %constant.92.clone) | copy-start | bytes 15364
  1953.0 11.7 copy-start.8
  (44 other events, 98.0 us)
